TPU v7x, 256 devices: a whole 4x4x8 slice. The times are simulated.
256 devices in a mesh: pair: 32 (over z, y), occ: 8 (over x, core).
Axes of the slice: x: 4, y: 4, z: 8, core: 2. Of those that a mesh axis runs over, the one named last changes fastest.
Arguments:
- amplitudes: float32 [256, 128, 128], P('pair'), may hold values from -4 to 4
- exchange_ints: float32 [256, 128, 128], P('pair'), may hold values from -6 to 6
- pno_energy: float32 [256, 128], P('pair'), may hold values from 0.3 to 3
- pair_shift: float32 [256], P('pair'), may hold values from 0.5 to 2
- coefficients: bfloat16 [256, 512, 128], P('pair'), may hold values from -0.5 to 0.5
- domain_tiles: int32 [256, 4], P('pair'), may hold values from 0 to 3, each once within a row
- couple_owner: int32 [8, 256, 8, 1], P('occ', 'pair'), may hold values from 0 to 31; in each aligned block of 64 rows (0 to 63, 64 to 127, ..., all dimensions but the last counted through in order) at most 3 rows name the same one
- couple_index: int32 [8, 256, 8], P('occ', 'pair'), may hold values from 0 to 7
- couple_weight: float32 [8, 256, 8], P('occ', 'pair'), may hold values from -0.5 to 0.5
Outputs:
- final_amplitudes: float32 [256, 128, 128], P('pair')
- final_residual: float32 [256, 128, 128], P('pair')
Inputs may be any that keep to these rules, and one draw needn't show every extreme that they name: `couple_owner`: among the couplings held by one device (one block of 64 entries), no owner is named more than 3 times. `domain_tiles`: the tiles of one pair's domain are distinct.
All inputs are finite; a program needn't handle non-finite values.
Results may differ from a plain program's by a relative error of at most 0.0003.
Values may be sent and summed in bfloat16 or wider, within the bound.
A program may use at most 128 MiB of HBM per device.

v0:
```python
import jax
import jax.numpy as jnp
from jax import lax
from jax.sharding import Mesh
from jax.sharding import PartitionSpec as P

ITERS = 2
PAIR = ("pair_0", "pair_1")
HIGHEST = lax.Precision.HIGHEST


def in_blocks(x, dim, peers):
    before, after = (x.shape[:dim], x.shape[dim + 1 :])
    return jnp.moveaxis(x.reshape(*before, peers, -1, *after), dim, 0)


def joined_along(pieces, dim):
    lengths = list(pieces.shape[1:])
    lengths[dim] *= pieces.shape[0]
    return jnp.moveaxis(pieces, 0, dim).reshape(lengths)


def moved_by_axis(pieces, axes, order):
    lengths = [lax.axis_size(a) for a in axes]
    pieces = pieces.reshape(*lengths, *pieces.shape[1:])
    for k in order:
        pieces = lax.all_to_all(pieces, axes[k], split_axis=k, concat_axis=k, tiled=True)
    return pieces.reshape(-1, *pieces.shape[len(axes) :])


def stepwise_exchange(x, axes, order, split_dim, concat_dim):
    pieces = in_blocks(x, split_dim, lax.axis_size(axes))
    return joined_along(moved_by_axis(pieces, axes, order), concat_dim)


def over_pieces(x, axis):
    pieces = lax.all_gather(x, axis)
    return pieces.sum(axis=0)


def local(
    amplitudes,
    exchange_ints,
    pno_energy,
    pair_shift,
    coefficients,
    domain_tiles,
    couple_owner,
    couple_index,
    couple_weight,
):
    pair_count = amplitudes.shape[0]
    pno_width = amplitudes.shape[1]
    domain = coefficients.shape[1]
    tile_count = domain_tiles.shape[1]
    couple_count = couple_index.shape[2]
    peer_count = lax.axis_size(PAIR)
    owners = couple_owner.reshape(-1)
    local_index = couple_index.reshape(-1)
    weights = couple_weight.reshape(pair_count, couple_count)
    total_count = owners.shape[0]
    capacity = max(2, 3 * total_count // (2 * peer_count))
    slot_total = peer_count * capacity
    position = jnp.arange(total_count, dtype=jnp.int32)
    same_owner = (owners[:, None] == owners[None, :]) & (position[None, :] < position[:, None])
    slot_rank = jnp.sum(same_owner.astype(jnp.int32), axis=1)
    slot_ids = owners * capacity + slot_rank
    requester_tiles = jnp.repeat(domain_tiles, couple_count, axis=0)
    payload = jnp.concatenate([local_index[:, None], requester_tiles], axis=1)
    requests = jnp.full((slot_total, 1 + tile_count), -1, jnp.int32).at[slot_ids].set(payload)
    arrived = stepwise_exchange(requests, PAIR, (0, 1), 0, 0)
    wanted = arrived[:, 0]
    their_tiles = arrived[:, 1:]
    pick_pair = wanted[:, None] == jnp.arange(pair_count, dtype=jnp.int32)[None, :]
    tile_match = their_tiles[:, :, None, None] == domain_tiles[None, None, :, :]
    selector = (pick_pair[:, None, :, None] & tile_match).astype(jnp.bfloat16)
    selector = selector.reshape(slot_total * tile_count, pair_count * tile_count)
    tile_blocks = coefficients.reshape(pair_count * tile_count, domain // tile_count * pno_width)
    moved_tiles = jnp.dot(selector, tile_blocks, preferred_element_type=jnp.float32).astype(
        jnp.bfloat16
    )
    moved_tiles = moved_tiles.reshape(slot_total, domain, pno_width)
    returned = lax.all_to_all(moved_tiles, PAIR, split_axis=0, concat_axis=0, tiled=True)
    their_coef = jnp.take(returned, slot_ids, axis=0).reshape(
        pair_count, couple_count, domain, pno_width
    )
    intersection = jnp.einsum(
        "pfa,pcfb->pcab", coefficients, their_coef, preferred_element_type=jnp.float32
    )
    denominator = pno_energy[:, :, None] + pno_energy[:, None, :] + pair_shift[:, None, None]
    global_ids = owners * pair_count + local_index
    current = amplitudes
    residual = amplitudes
    for iteration in range(ITERS):
        all_amps = lax.all_gather(current, PAIR, axis=0, tiled=True)
        partner_amp = jnp.take(all_amps, global_ids, axis=0)
        partner_amp = partner_amp.reshape(pair_count, couple_count, pno_width, pno_width)
        inner_prod = jnp.einsum("pcab,pcbd->pcad", intersection, partner_amp, precision=HIGHEST)
        outer_prod = jnp.einsum("pcad,pced->pcae", inner_prod, intersection, precision=HIGHEST)
        partial_value = jnp.einsum("pc,pcae->pae", weights, outer_prod, precision=HIGHEST)
        coupled = over_pieces(partial_value, "occ")
        residual = exchange_ints + denominator * current - coupled
        current = current - residual / denominator
    return (current, residual)


def solution(mesh):
    split = Mesh(mesh.devices.reshape(8, 4, mesh.shape["occ"]), ("pair_0", "pair_1", "occ"))
    in_specs = (
        P(PAIR, None, None),
        P(PAIR, None, None),
        P(PAIR, None),
        P(PAIR),
        P(PAIR, None, None),
        P(PAIR, None),
        P("occ", PAIR, None, None),
        P("occ", PAIR, None),
        P("occ", PAIR, None),
    )
    out_specs = (P(PAIR, None, None), P(PAIR, None, None))
    return jax.shard_map(local, mesh=split, in_specs=in_specs, out_specs=out_specs, check_vma=False)
```

profile of v0, /device:TPU:1, one launch (start us, length us, event | category | flops | bytes accessed | tf_op | source)
XLA Modules:
  0.0 751.8 jit_solution(6762921172561022608)
XLA Ops:
  13.3 15.9 %all_to_all.15 = s32[8,4,3,5]{3,1,2,0:T(4,128)S(1)} all-to-all(s32[8,4,3,5]{3,1,2,0:T(4,128)S(1)} %copy.36), channel_id=1, replica_groups=mesh['pair_0'=8,'pair_1'=4,'occ'=8] {'pair_0'}, dimensions={0} | all-to-all | bytes 3840 | tf_op jit(solution)/shard_map/all_to_all | solution.py:27
  30.0 4.2 all-to-all-start.1
  40.9 6.4 convolution_convert_fusion
  47.3 19.6 %reshape.165 = bf16[96,512,128]{2,1,0:T(8,128)(2,1)} reshape(bf16[384,16384]{1,0:T(8,128)(2,1)} %convolution_convert_fusion) | data formatting | bytes 25165824 | tf_op jit(solution)/shard_map/reshape | solution.py:82
  66.9 5.2 all-to-all-start.2
  72.4 351.0 %all-to-all-done.2 = bf16[96,512,128]{2,1,0:T(8,128)(2,1)} async-done(((bf16[96,512,128]{2,1,0:T(8,128)(2,1)}), bf16[96,512,128]{2,1,0:T(8,128)(2,1)}, u32[]{:S(2)}, u32[]{:S(2)}) %all-to-all-start.2) | async-done | bytes 12582944 | tf_op jit(solution)/shard_map/all_to_all | solution.py:83
  423.4 10.2 %gather_fusion = bf16[64,512,128]{2,1,0:T(8,128)(2,1)} fusion(bf16[96,512,128]{2,1,0:T(8,128)(2,1)} %all-to-all-done.2, s32[1024]{0:T(1024)S(1)} %pad_clamp_fusion.1), kind=kCustom, calls=%fused_computation.2 | custom fusion | bytes 16777472 | tf_op jit(solution)/shard_map/jit(_take)/gather | solution.py:84
  433.6 12.2 %copy.41 = bf16[64,512,128]{1,2,0:T(8,128)(2,1)} copy(bf16[64,512,128]{2,1,0:T(8,128)(2,1)} %gather_fusion) | data formatting | bytes 16777216 | tf_op jit(solution)/shard_map/jit(_take)/gather | solution.py:84
  445.8 7.7 %fusion = f32[8,8,128,128]{3,2,1,0:T(8,128)} fusion(bf16[8,8,512,128]{2,3,1,0:T(8,128)(2,1)} %bitcast.63, pred[8,8]{1,0:T(8,128)(4,1)S(1)} %compare_and_fusion.1, bf16[8,512,128]{2,1,0:T(8,128)(2,1)S(1)} %copy-done.6), kind=kOutput, calls=%fused_computation.5 | convolution fusion | flops 1077936128 | bytes 13631552 | tf_op jit(solution)/shard_map/pfa,pcfb->pcab/dot_general | solution.py:87
  453.6 8.5 %gather_fusion.1 = f32[64,128,128]{2,1,0:T(8,128)} fusion(f32[256,128,128]{2,1,0:T(8,128)} %all-gather.7.cloned.1.call-done, s32[1024]{0:T(1024)S(1)} %pad_clamp_fusion), kind=kCustom, calls=%fused_computation.clone | custom fusion | bytes 8388864 | tf_op jit(solution)/shard_map/jit(_take)/gather | solution.py:96
  462.1 2.7 broadcast_select_fusion.1
  465.6 7.3 fusion.14
  472.9 5.8 fusion.15
  478.8 6.1 fusion.5
  484.9 48.7 %all-gather.11.cloned.1.call-done = f32[64,128,128]{2,1,0:T(8,128)} async-done(((f32[8,128,128]{2,1,0:T(8,128)}), f32[64,128,128]{2,1,0:T(8,128)}) %all-gather.11.cloned.1.call-update) | async-done | bytes 4194320 | tf_op jit(solution)/shard_map/all_gather | solution.py:37
  533.6 2.5 reduce_sum.34
  537.2 139.9 %all-gather.9.cloned.1.call-done = f32[256,128,128]{2,1,0:T(8,128)} async-done(((f32[8,128,128]{2,1,0:T(8,128)}), f32[256,128,128]{2,1,0:T(8,128)}) %all-gather.9.cloned.1.call-update) | async-done | bytes 16777232 | tf_op jit(solution)/shard_map/all_gather | solution.py:95
  677.2 8.5 %gather_fusion.2 = f32[64,128,128]{2,1,0:T(8,128)} fusion(f32[256,128,128]{2,1,0:T(8,128)} %all-gather.9.cloned.1.call-done, s32[1024]{0:T(1024)S(1)} %pad_clamp_fusion), kind=kCustom, calls=%fused_computation.1.clone | custom fusion | bytes 8388864 | tf_op jit(solution)/shard_map/jit(_take)/gather | solution.py:96
  685.7 2.7 broadcast_select_fusion
  689.1 7.3 fusion.16
  696.4 5.9 fusion.17
  702.3 6.1 fusion.3
  708.4 32.6 %all-gather.13.cloned.1.call-done = f32[64,128,128]{2,1,0:T(8,128)} async-done(((f32[8,128,128]{2,1,0:T(8,128)}), f32[64,128,128]{2,1,0:T(8,128)}) %all-gather.13.cloned.1.call-update) | async-done | bytes 4194320 | tf_op jit(solution)/shard_map/all_gather | solution.py:37
  741.1 2.5 reduce_sum.35
  (66 shorter events, 17.7 us)
Async XLA Ops:
  7.2 471.5 %copy-start = (f32[1,8,8]{2,1,0:T(8,128)S(1)}, f32[1,8,8]{2,1,0:T(8,128)}, u32[]{:S(2)}) copy-start(f32[1,8,8]{2,1,0:T(8,128)} %param.19) | copy-start | bytes 772
  7.2 446.4 %all-gather.7.cloned.1.call-start = ((), (), s32[]{:S(2)}) async-start(), calls=%async_computation.3 | async-start | bytes 17301504 | tf_op jit(solution)/shard_map/all_gather | solution.py:95
  30.0 8.8 %all-to-all-start.1 = ((s32[8,4,3,5]{0,2,3,1:T(4,128)}), s32[8,4,3,5]{0,2,3,1:T(4,128)S(1)}, u32[]{:S(2)}, u32[]{:S(2)}) async-start(s32[8,4,3,5]{0,2,3,1:T(4,128)} %copy.37), calls=%async_computation.1 | async-start | bytes 81920 | tf_op jit(solution)/shard_map/all_to_all | solution.py:27
  66.9 5.4 copy-start.9
  66.9 5.5 copy-start.8
  66.9 356.5 %all-to-all-start.2 = ((bf16[96,512,128]{2,1,0:T(8,128)(2,1)}), bf16[96,512,128]{2,1,0:T(8,128)(2,1)}, u32[]{:S(2)}, u32[]{:S(2)}) async-start(bf16[96,512,128]{2,1,0:T(8,128)(2,1)} %reshape.165), calls=%async_computation.2 | async-start | bytes 25165824 | tf_op jit(solution)/shard_map/all_to_all | solution.py:83
  72.2 461.4 %all-gather.11.cloned.1.call-start = ((), (), s32[]{:S(2)}) async-start(), calls=%async_computation.5 | async-start | bytes 4718592 | tf_op jit(solution)/shard_map/all_gather | solution.py:37
  433.6 12.2 %copy-start.6 = (bf16[8,512,128]{2,1,0:T(8,128)(2,1)S(1)}, bf16[8,512,128]{2,1,0:T(8,128)(2,1)}, u32[]{:S(2)}) copy-start(bf16[8,512,128]{2,1,0:T(8,128)(2,1)} %param.15) | copy-start | bytes 3145732
  462.1 3.4 copy-start.1
  478.7 57.4 %copy-start.4 = (f32[8,128,128]{2,1,0:T(8,128)S(1)}, f32[8,128,128]{2,1,0:T(8,128)}, u32[]{:S(2)}) copy-start(f32[8,128,128]{2,1,0:T(8,128)} %param.11) | copy-start | bytes 1572868
  478.7 57.4 %copy-start.5 = (f32[8,128,128]{2,1,0:T(8,128)S(1)}, f32[8,128,128]{2,1,0:T(8,128)}, u32[]{:S(2)}) copy-start(f32[8,128,128]{2,1,0:T(8,128)} %param.12) | copy-start | bytes 1572868
  478.7 57.4 %copy-start.7 = (f32[8,128]{1,0:T(8,128)S(1)}, f32[8,128]{1,0:T(8,128)}, u32[]{:S(2)}) copy-start(f32[8,128]{1,0:T(8,128)} %param.13) | copy-start | bytes 12292
  478.7 57.4 %copy-start.10 = (f32[8]{0:T(128)S(1)}, f32[8]{0:T(128)}, u32[]{:S(2)}) copy-start(f32[8]{0:T(128)} %param.14) | copy-start | bytes 100
  484.9 192.3 %all-gather.9.cloned.1.call-start = ((), (), s32[]{:S(2)}) async-start(), calls=%async_computation.4 | async-start | bytes 17301504 | tf_op jit(solution)/shard_map/all_gather | solution.py:95
  537.2 203.9 %all-gather.13.cloned.1.call-start = ((), (), s32[]{:S(2)}) async-start(), calls=%async_computation.6 | async-start | bytes 4718592 | tf_op jit(solution)/shard_map/all_gather | solution.py:37
  685.7 3.4 copy-start.2
  702.3 41.3 %copy-start.3 = (f32[8,128,128]{2,1,0:T(8,128)S(1)}, f32[8,128,128]{2,1,0:T(8,128)}, u32[]{:S(2)}) copy-start(f32[8,128,128]{2,1,0:T(8,128)} %divide_subtract_fusion.1) | copy-start | bytes 1572868
Sparse Core Ops, SparseCore 0:
  10.6 325.4 all-gather.6
  485.0 48.5 all-gather.10
  537.3 139.8 all-gather.8
  708.6 32.4 all-gather.12
where the time goes:
time: 758 us; the launch traced here: 752 us
  waiting for transfers between devices  575 us (76%)
  local copies, waits for them, and re-layouts  68.8 us (9%)
  matrix products  52.6 us (7%)
  blocking collectives  15.9 us (2%)
  other arithmetic  15.2 us (2%)
  between operations  14.5 us (2%)
  starting transfers between devices  9.56 us (1%)
    all_to_all x1, waiting for transfers between devices, local(): lax.all_to_all(moved_tiles, PAIR, split_axis=0, concat_axis=0, tiled=True)  351 us
    all_gather x2, waiting for transfers between devices, local(): all_amps = lax.all_gather(current, PAIR, axis=0, tiled=True)  140 us
    all_gather x2, waiting for transfers between devices, over_pieces(): pieces = lax.all_gather(x, axis)  81.3 us
    gather x2, local copies, waits for them, and re-layouts, local(): jnp.take(returned, slot_ids, axis=0)  22.4 us
    reshape x1, local copies, waits for them, and re-layouts, local(): moved_tiles = moved_tiles.reshape(slot_total, domain, pno_width)  19.6 us
    gather x2, local copies, waits for them, and re-layouts, local(): partner_amp = jnp.take(all_amps, global_ids, axis=0)  17.1 us
    all_to_all x1, blocking collectives, moved_by_axis(): lax.all_to_all(pieces, axes[k], split_axis=k, concat_axis=k, tiled=True)  15.9 us
  transfers between devices with their start and end apart: 6, of which 5 were waited for; matrix products, arithmetic and copies ran while one was open for 9% of the time, Pallas kernels for 0%

commit v1 on v0

--- a/solution.py
+++ b/solution.py
@@ -92,7 +92,10 @@
     current = amplitudes
     residual = amplitudes
     for iteration in range(ITERS):
-        all_amps = lax.all_gather(current, PAIR, axis=0, tiled=True)
+        size = lax.axis_size(PAIR)
+        shards = jnp.stack([current for _ in range(size)])
+        shards = lax.all_to_all(shards, PAIR, split_axis=0, concat_axis=0)
+        all_amps = jnp.concatenate(shards, axis=0)
         partner_amp = jnp.take(all_amps, global_ids, axis=0)
         partner_amp = partner_amp.reshape(pair_count, couple_count, pno_width, pno_width)
         inner_prod = jnp.einsum("pcab,pcbd->pcad", intersection, partner_amp, precision=HIGHEST)

time: 758 us -> 1270 us (1.68)
  blocking collectives: 15.9 us -> 666 us
  waiting for transfers between devices: 575 us -> 424 us
    all_to_all x0 -> x2, blocking collectives: none -> 650 us  [the longest x1 373 us: local(): shards = lax.all_to_all(shards, PAIR, split_axis=0, concat_axis=0)]
    all_gather x2 -> x0, waiting for transfers between devices: 140 us -> none  [local(): all_amps = lax.all_gather(current, PAIR, axis=0, tiled=True)]
    all_to_all x1, waiting for transfers between devices: 351 us -> 334 us  [local(): shards = lax.all_to_all(shards, PAIR, split_axis=0, concat_axis=0)]
  transfers between devices with their start and end apart: 6 -> 4, of which waited for: 5 -> 4; matrix products, arithmetic and copies ran while one was open for 9% -> 3% of each run, Pallas kernels for 0% -> 0%
where the time goes in v1:
time: 1270 us; the launch traced here: 1260 us
  blocking collectives  666 us (52%)
  waiting for transfers between devices  424 us (33%)
  local copies, waits for them, and re-layouts  78.6 us (6%)
  matrix products  52.5 us (4%)
  between operations  14.8 us (1%)
  other arithmetic  14.4 us (1%)
    all_to_all x1, blocking collectives, local(): shards = lax.all_to_all(shards, PAIR, split_axis=0, concat_axis=0)  373 us
    all_to_all x1, waiting for transfers between devices, local(): shards = lax.all_to_all(shards, PAIR, split_axis=0, concat_axis=0)  334 us
    all_to_all x1, blocking collectives, local(): lax.all_to_all(moved_tiles, PAIR, split_axis=0, concat_axis=0, tiled=True)  276 us
    all_gather x2, waiting for transfers between devices, over_pieces(): pieces = lax.all_gather(x, axis)  87.3 us
  transfers between devices with their start and end apart: 4, of which 4 were waited for; matrix products, arithmetic and copies ran while one was open for 3% of the time, Pallas kernels for 0%

profile of v1, /device:TPU:1, one launch (start us, length us, event | category | flops | bytes accessed | tf_op | source)
XLA Modules:
  0.0 1260.7 jit_solution(2455443069356914828)
XLA Ops:
  12.6 15.9 %all_to_all.25 = s32[8,4,3,5]{3,1,2,0:T(4,128)S(1)} all-to-all(s32[8,4,3,5]{3,1,2,0:T(4,128)S(1)} %copy.36), channel_id=1, replica_groups=mesh['pair_0'=8,'pair_1'=4,'occ'=8] {'pair_0'}, dimensions={0} | all-to-all | bytes 3840 | tf_op jit(solution)/shard_map/all_to_all | solution.py:27
  29.3 4.2 all-to-all-start.1
  39.9 6.3 convolution_convert_fusion
  46.2 19.5 %reshape.175 = bf16[96,512,128]{2,1,0:T(8,128)(2,1)} reshape(bf16[384,16384]{1,0:T(8,128)(2,1)} %convolution_convert_fusion) | data formatting | bytes 25165824 | tf_op jit(solution)/shard_map/reshape | solution.py:82
  65.8 276.4 %all_to_all.26 = bf16[96,512,128]{2,1,0:T(8,128)(2,1)} all-to-all(bf16[96,512,128]{2,1,0:T(8,128)(2,1)} %reshape.175), channel_id=1, replica_groups=mesh['pair_0'=8,'pair_1'=4,'occ'=8] {'pair_0','pair_1'}, dimensions={0} | all-to-all | bytes 25165824 | tf_op jit(solution)/shard_map/all_to_all | solution.py:83
  342.1 7.9 stack.4
  350.0 6.9 all-to-all-start.3
  357.2 10.2 gather_fusion
  367.4 12.2 copy.41
  379.6 7.7 fusion
  387.3 334.3 %all-to-all-done.3 = f32[32,8,128,128]{3,2,1,0:T(8,128)} async-done(((f32[32,8,128,128]{3,2,1,0:T(8,128)}), f32[32,8,128,128]{3,2,1,0:T(8,128)}, u32[]{:S(2)}, u32[]{:S(2)}) %all-to-all-start.3) | async-done | bytes 16777248 | tf_op jit(solution)/shard_map/all_to_all | solution.py:97
  721.6 8.5 gather_fusion.1
  730.1 2.7 broadcast_select_fusion.1
  733.6 7.3 fusion.14
  740.8 5.8 fusion.15
  746.7 6.1 fusion.5
  752.9 54.9 %all-gather.5.cloned.1.call-done = f32[64,128,128]{2,1,0:T(8,128)} async-done(((f32[8,128,128]{2,1,0:T(8,128)}), f32[64,128,128]{2,1,0:T(8,128)}) %all-gather.5.cloned.1.call-update) | async-done | bytes 4194320 | tf_op jit(solution)/shard_map/all_gather | solution.py:37
  812.6 373.4 %all_to_all.27 = f32[32,8,128,128]{3,2,1,0:T(8,128)} all-to-all(f32[32,8,128,128]{3,2,1,0:T(8,128)S(1)} %stack.5), channel_id=1, replica_groups=mesh['pair_0'=8,'pair_1'=4,'occ'=8] {'pair_0','pair_1'}, dimensions={0} | all-to-all | bytes 33554432 | tf_op jit(solution)/shard_map/all_to_all | solution.py:97
  1186.0 8.5 gather_fusion.2
  1194.6 2.7 broadcast_select_fusion
  1198.0 7.3 fusion.16
  1205.3 5.9 fusion.17
  1211.2 6.1 fusion.3
  1217.3 32.4 %all-gather.7.cloned.1.call-done = f32[64,128,128]{2,1,0:T(8,128)} async-done(((f32[8,128,128]{2,1,0:T(8,128)}), f32[64,128,128]{2,1,0:T(8,128)}) %all-gather.7.cloned.1.call-update) | async-done | bytes 4194320 | tf_op jit(solution)/shard_map/all_gather | solution.py:37
  (62 shorter events, 23.0 us)
Async XLA Ops:
  7.2 739.5 %copy-start = (f32[1,8,8]{2,1,0:T(8,128)S(1)}, f32[1,8,8]{2,1,0:T(8,128)}, u32[]{:S(2)}) copy-start(f32[1,8,8]{2,1,0:T(8,128)} %param.19) | copy-start | bytes 772
  29.3 8.5 all-to-all-start.1
  65.8 276.4 %copy-start.3 = (f32[8,128,128]{2,1,0:T(8,128)S(1)}, f32[8,128,128]{2,1,0:T(8,128)}, u32[]{:S(2)}) copy-start(f32[8,128,128]{2,1,0:T(8,128)} %param.11) | copy-start | bytes 1572868
  350.0 7.0 copy-start.8
  350.0 7.2 copy-start.7
  350.0 371.6 %all-to-all-start.3 = ((f32[32,8,128,128]{3,2,1,0:T(8,128)}), f32[32,8,128,128]{3,2,1,0:T(8,128)}, u32[]{:S(2)}, u32[]{:S(2)}) async-start(f32[32,8,128,128]{3,2,1,0:T(8,128)} %stack.4), calls=%async_computation.3 | async-start | bytes 33554432 | tf_op jit(solution)/shard_map/all_to_all | solution.py:97
  356.9 450.8 %all-gather.5.cloned.1.call-start = ((), (), s32[]{:S(2)}) async-start(), calls=%async_computation.5 | async-start | bytes 4718592 | tf_op jit(solution)/shard_map/all_gather | solution.py:37
  367.4 12.2 copy-start.5
  730.1 3.4 copy-start.1
  746.7 63.6 %copy-start.4 = (f32[8,128,128]{2,1,0:T(8,128)S(1)}, f32[8,128,128]{2,1,0:T(8,128)}, u32[]{:S(2)}) copy-start(f32[8,128,128]{2,1,0:T(8,128)} %param.12) | copy-start | bytes 1572868
  746.7 63.6 %copy-start.6 = (f32[8,128]{1,0:T(8,128)S(1)}, f32[8,128]{1,0:T(8,128)}, u32[]{:S(2)}) copy-start(f32[8,128]{1,0:T(8,128)} %param.13) | copy-start | bytes 12292
  746.7 63.5 %copy-start.9 = (f32[8]{0:T(128)S(1)}, f32[8]{0:T(128)}, u32[]{:S(2)}) copy-start(f32[8]{0:T(128)} %param.14) | copy-start | bytes 100
  752.8 496.9 %all-gather.7.cloned.1.call-start = ((), (), s32[]{:S(2)}) async-start(), calls=%async_computation.6 | async-start | bytes 4718592 | tf_op jit(solution)/shard_map/all_gather | solution.py:37
  1194.5 3.4 copy-start.2
Sparse Core Ops, SparseCore 0:
  753.0 54.7 all-gather.4
  1217.4 32.2 all-gather.6
